TPU v7x, 512 devices: a whole 4x8x8 slice. The times are simulated.
512 devices in a mesh: dp: 32 (over z, y_hi), segment: 2 (over y_lo), mp: 8 (over x, core).
Axes of the slice: x: 4, y: 8 (y_hi: 4, y_lo: 2; y = y_hi * 2 + y_lo), z: 8, core: 2. Of those that a mesh axis runs over, the one named last changes fastest.
Arguments:
- prefix_hidden: bfloat16 [64, 512, 8192], P(('dp', 'segment'), 'mp'), may hold values from -16 to 16
- norm_gain: float32 [8192], replicated, may hold values from 0.5 to 1.5
- kv_weight: bfloat16 [8192, 2, 1024], P('dp', None, 'mp'), may hold values from -0.0625 to 0.0625
- action_query: bfloat16 [64, 128, 2048], P(('dp', 'segment'), None, 'mp'), may hold values from -104 to 104
- action_kv: bfloat16 [64, 128, 2, 1024], P(('dp', 'segment'), None, None, 'mp'), may hold values from -4.25 to 4.25
- out_cotangent: bfloat16 [64, 128, 2048], P(('dp', 'segment'), None, 'mp'), may hold values from -18 to 18
- prefix_blocks: int32 [64, 512], P(('dp', 'segment')), may hold values from 0 to 7, as said below
- action_blocks: int32 [64, 128], P(('dp', 'segment')), may hold values from 0 to 8, as said below
- prefix_lengths: int32 [64], P(('dp', 'segment')), may hold values from 128 to 512, as said below
- timesteps: int32 [64], P(('dp', 'segment')), may hold values from 0 to 999
Outputs:
- attn_out: bfloat16 [64, 128, 2048], P(('dp', 'segment'), None, 'mp')
- query_grad: float32 [64, 128, 2048], P(('dp', 'segment'), None, 'mp')
- action_kv_grad: float32 [64, 128, 2, 1024], P(('dp', 'segment'), None, None, 'mp')
- weight_grad: float32 [8192, 2, 1024], P('dp', None, 'mp')
Inputs may be any that keep to these rules, and one draw needn't show every extreme that they name: `prefix_blocks`: constant over each run of 64 positions, 0 on the first run, rising by 0 or 1 from one run to the next; in every draw some sample rises at every run. `action_blocks`: constant over each run of 64 positions; the last run of every sample holds 8; in every draw some sample's first run holds 0. `prefix_lengths`: in every draw some sample's prefix is whole and some sample's is 128.
All inputs are finite; a program needn't handle non-finite values.
Results may differ from a plain program's by a relative error of at most 0.017.
Values may be sent and summed in bfloat16 or wider, within the bound.
No kernel may reach another device: no remote copies, remote signals or barrier semaphores. Data moves between devices by JAX's collectives and lax.ppermute only.
A program may use at most 64 MiB of HBM per device.

v0:
```python
import jax
import jax.numpy as jnp
from jax import lax
from jax.sharding import Mesh
from jax.sharding import PartitionSpec as P

KVH = 8
HD = 128
QH = 16
STEPS = 1000
DP = ("dp_0", "dp_1")
DP_SEGMENT = ("dp_0", "dp_1", "segment")
EPS = 1e-06
NEGATIVE = -1e30


def sum_by_axis(terms, axes):
    subtotal = terms.astype(jnp.bfloat16)
    for axis in axes:
        subtotal = lax.psum_scatter(subtotal, axis, scatter_dimension=0, tiled=True)
    return subtotal.astype(jnp.float32)


def from_everyone(array, axis):
    copies = jnp.broadcast_to(array, (lax.axis_size(axis), *array.shape))
    return lax.all_to_all(copies, axis, split_axis=0, concat_axis=0, tiled=True)


def taken_together(array, axis):
    everything = from_everyone(array, axis)
    return jnp.sum(everything.astype(jnp.float32), axis=0)


def head_scores(query, keys):
    return jnp.einsum("agrh,jgh->graj", query, keys, preferred_element_type=jnp.float32) * HD ** (
        -0.5
    )


def backward_terms(probs, values, keys, query, grad_out):
    probs_low = probs.astype(jnp.bfloat16)
    d_probs = jnp.einsum("agrh,jgh->graj", grad_out, values, preferred_element_type=jnp.float32)
    delta = jnp.sum(probs * d_probs, axis=-1, keepdims=True)
    d_scores = (probs * (d_probs - delta)).astype(jnp.bfloat16)
    d_query = jnp.einsum(
        "graj,jgh->agrh", d_scores, keys, preferred_element_type=jnp.float32
    ) * HD ** (-0.5)
    d_keys = jnp.einsum(
        "graj,agrh->jgh", d_scores, query, preferred_element_type=jnp.float32
    ) * HD ** (-0.5)
    d_values = jnp.einsum("graj,agrh->jgh", probs_low, grad_out, preferred_element_type=jnp.float32)
    return (d_query, jnp.stack([d_keys, d_values], axis=1))


def shards(
    prefix_hidden,
    norm_gain,
    kv_weight,
    action_query,
    action_kv,
    out_cotangent,
    prefix_blocks,
    action_blocks,
    prefix_lengths,
    timesteps,
):
    acts = action_query.shape[1]
    heads_kv = kv_weight.shape[2] // HD
    ratio = QH // KVH
    columns = 2 * kv_weight.shape[2]
    wide = prefix_hidden[0].astype(jnp.float32)
    inverse = lax.rsqrt(jnp.mean(wide * wide, axis=-1, keepdims=True) + EPS)
    normed_local = (wide * inverse * norm_gain).astype(jnp.bfloat16)
    normed = lax.all_gather(normed_local, "mp", axis=0, tiled=True)
    rows = normed.shape[0]
    piece = lax.all_gather(kv_weight, DP, axis=0, tiled=True)
    section = normed
    projected = jnp.dot(
        section, piece.reshape(piece.shape[0], columns), preferred_element_type=jnp.float32
    )
    prefix_kv = projected.astype(jnp.bfloat16).reshape(rows, 2, heads_kv, HD)
    own_pair = action_kv[0].reshape(acts, 2, heads_kv, HD)
    query = action_query[0].reshape(acts, heads_kv, ratio, HD)
    flow_weight = 0.5 + (timesteps[0].astype(jnp.float32) + 0.5) / STEPS
    grad_out = (
        (flow_weight * out_cotangent[0].astype(jnp.float32))
        .astype(jnp.bfloat16)
        .reshape(acts, heads_kv, ratio, HD)
    )
    pblocks = prefix_blocks[0]
    ablocks = action_blocks[0]
    length = prefix_lengths[0]
    keys = jnp.concatenate([prefix_kv[:, 0], own_pair[:, 0]], axis=0)
    values = jnp.concatenate([prefix_kv[:, 1], own_pair[:, 1]], axis=0)
    positions = jnp.arange(rows, dtype=jnp.int32)
    see_prefix = (pblocks[None, :] <= ablocks[:, None]) & (positions[None, :] < length)
    see_action = ablocks[None, :] <= ablocks[:, None]
    visible = jnp.concatenate([see_prefix, see_action], axis=1)
    masked = jnp.where(visible, head_scores(query, keys), NEGATIVE)
    top = jnp.max(masked, axis=-1, keepdims=True)
    expo = jnp.where(visible, jnp.exp(masked - top), 0.0)
    probs = expo / jnp.sum(expo, axis=-1, keepdims=True)
    out = jnp.einsum(
        "graj,jgh->agrh", probs.astype(jnp.bfloat16), values, preferred_element_type=jnp.float32
    )
    d_query, d_pair = backward_terms(probs, values, keys, query, grad_out)
    d_prefix = d_pair[:rows]
    d_action = d_pair[rows:]
    attn_out = out.astype(jnp.bfloat16).reshape(1, acts, ratio * heads_kv * HD)
    query_grad = d_query.reshape(1, acts, ratio * heads_kv * HD)
    action_kv_grad = d_action.reshape(1, acts, 2, heads_kv * HD)
    prefix_grad = d_prefix.astype(jnp.bfloat16).reshape(rows, columns)
    section = normed
    term = lax.dot_general(
        section, prefix_grad, (((0,), (0,)), ((), ())), preferred_element_type=jnp.float32
    )
    shard = sum_by_axis(term.reshape(kv_weight.shape[0] * lax.axis_size(DP), 2, columns // 2), DP)
    weight_grad = taken_together(shard.astype(jnp.bfloat16), "segment").astype(jnp.float32)
    return (attn_out, query_grad, action_kv_grad, weight_grad)


def solution(mesh):
    torus = Mesh(
        mesh.devices.reshape(8, 4, mesh.shape["segment"], mesh.shape["mp"]),
        ("dp_0", "dp_1", "segment", "mp"),
    )
    placed = (
        P(DP_SEGMENT, "mp", None),
        P(),
        P(DP, None, "mp"),
        P(DP_SEGMENT, None, "mp"),
        P(DP_SEGMENT, None, None, "mp"),
        P(DP_SEGMENT, None, "mp"),
        P(DP_SEGMENT, None),
        P(DP_SEGMENT, None),
        P(DP_SEGMENT),
        P(DP_SEGMENT),
    )
    return jax.shard_map(
        shards,
        mesh=torus,
        in_specs=placed,
        out_specs=(
            P(DP_SEGMENT, None, "mp"),
            P(DP_SEGMENT, None, "mp"),
            P(DP_SEGMENT, None, None, "mp"),
            P(DP, None, "mp"),
        ),
        check_vma=False,
    )
```

profile of v0, /device:TPU:18, one launch (start us, length us, event | category | flops | bytes accessed | tf_op | source)
XLA Modules:
  0.0 294.3 jit_solution(14425961718619464857)
XLA Ops:
  7.2 0.0 copy-start
  7.2 0.0 copy-start.1
  7.2 0.0 copy-start.2
  7.2 0.0 copy-start.3
  7.2 0.0 copy-start.4
  7.2 0.0 all-gather.5.cloned.1.call-start
  7.3 0.7 all-gather.5.cloned.1.call-update
  8.0 0.0 all-gather.3.cloned.1.call-start
  8.0 1.5 fusion.4
  9.5 2.6 fusion.6
  12.1 0.0 all-gather.3.cloned.1.call-update
  12.2 0.0 reduce-scatter.3.cloned.1.call-start
  12.2 0.0 copy-done
  12.2 0.1 copy.52
  12.4 0.0 copy-done.1
  12.4 0.1 copy.77
  13.8 0.0 copy-done.2
  13.8 0.1 copy.78
  14.0 0.0 copy-done.3
  14.0 0.1 broadcast_compare_fusion
  14.1 0.0 copy-done.4
  14.1 0.2 compare_and_fusion
  14.3 102.6 %all-gather.5.cloned.1.call-done = bf16[8192,2,128]{2,1,0:T(2,128)(2,1)} async-done(((bf16[256,2,128]{2,1,0:T(2,128)(2,1)}), bf16[8192,2,128]{2,1,0:T(2,128)(2,1)}) %all-gather.5.cloned.1.call-update) | async-done | bytes 4194320 | tf_op jit(solution)/shard_map/all_gather | solution.py:76
  116.9 54.1 %all-gather.3.cloned.1.call-done = bf16[512,8192]{1,0:T(8,128)(2,1)} async-done(((bf16[64,8192]{1,0:T(8,128)(2,1)}), bf16[512,8192]{1,0:T(8,128)(2,1)}) %all-gather.3.cloned.1.call-update) | async-done | bytes 8388624 | tf_op jit(solution)/shard_map/all_gather | solution.py:74
  170.9 6.9 %fusion.8 = bf16[512,256]{0,1:T(8,128)(2,1)S(1)} fusion(bf16[512,8192]{1,0:T(8,128)(2,1)} %all-gather.3.cloned.1.call-done, bf16[1024,8,2,128]{3,2,1,0:T(2,128)(2,1)} %bitcast.129), kind=kOutput, calls=%fused_computation.13 | convolution fusion | flops 2147614720 | bytes 12845056 | tf_op jit(solution)/shard_map/dot_general | solution.py:78
  177.9 0.1 copy.76
  178.0 0.3 fusion.33
  178.3 0.1 fusion.15
  178.5 0.0 copy-start.5
  178.5 0.3 convolution_bitcast_fusion.1
  178.8 0.3 multiply_reduce_fusion
  179.1 0.2 fusion.17
  179.3 0.2 fusion.13
  179.6 2.3 copy-done.5
  181.8 4.0 %convolution_convert_fusion = bf16[8192,2,128]{2,0,1:T(8,128)(2,1)} fusion(bf16[512,8192]{1,0:T(8,128)(2,1)S(1)} %copy-done.5, f32[640,1,1,128]{0,3,2,1:T(8,128)S(1)} %convolution_bitcast_fusion.1, f32[640,1,1,128]{0,3,2,1:T(8,128)S(1)} %fusion.13), kind=kOutput, calls=%fused_computation | convolution fusion | flops 2150105088 | bytes 13238272 | tf_op jit(solution)/shard_map/dot_general | solution.py:114
  185.8 0.0 reduce-scatter.3.cloned.1.call-update
  185.8 0.0 reduce-scatter.5.cloned.1.call-start
  185.9 59.9 %reduce-scatter.3.cloned.1.call-done = bf16[1024,2,128]{2,0,1:T(8,128)(2,1)} async-done(((bf16[8192,2,128]{2,0,1:T(8,128)(2,1)}), bf16[1024,2,128]{2,0,1:T(8,128)(2,1)}) %reduce-scatter.3.cloned.1.call-update) | async-done | bytes 524304 | tf_op jit(solution)/shard_map/reduce_scatter | solution.py:20
  245.7 0.0 reduce-scatter.5.cloned.1.call-update
  245.8 0.3 convolution_convert_fusion.1
  246.1 0.7 copy.64
  246.8 29.7 %reduce-scatter.5.cloned.1.call-done = bf16[256,2,128]{2,0,1:T(8,128)(2,1)} async-done(((bf16[1024,2,128]{2,0,1:T(8,128)(2,1)}), bf16[256,2,128]{2,0,1:T(8,128)(2,1)}) %reduce-scatter.5.cloned.1.call-update) | async-done | bytes 131088 | tf_op jit(solution)/shard_map/reduce_scatter | solution.py:20
  276.6 1.6 broadcast_in_dim.24
  278.2 3.4 %all-to-all-start = ((bf16[2,256,2,128]{3,1,2,0:T(8,128)(2,1)}), bf16[2,256,2,128]{3,1,2,0:T(8,128)(2,1)S(1)}, u32[]{:S(2)}, u32[]{:S(2)}) async-start(bf16[2,256,2,128]{3,1,2,0:T(8,128)(2,1)} %broadcast_in_dim.24), calls=%async_computation.2 | async-start | bytes 524288 | tf_op jit(solution)/shard_map/all_to_all | solution.py:26
  281.7 0.3 convolution_multiply_fusion.1
  281.9 0.8 copy.65
  282.7 0.8 copy.66
  283.4 3.4 %all-to-all-done = bf16[2,256,2,128]{3,1,2,0:T(8,128)(2,1)S(1)} async-done(((bf16[2,256,2,128]{3,1,2,0:T(8,128)(2,1)}), bf16[2,256,2,128]{3,1,2,0:T(8,128)(2,1)S(1)}, u32[]{:S(2)}, u32[]{:S(2)}) %all-to-all-start) | async-done | bytes 262176 | tf_op jit(solution)/shard_map/all_to_all | solution.py:26
  286.8 0.9 copy.67
  (10 shorter events, 0.1 us)
Async XLA Ops:
  7.2 5.0 %copy-start = (bf16[1,128,2,128]{3,2,1,0:T(2,128)(2,1)S(1)}, bf16[1,128,2,128]{3,2,1,0:T(2,128)(2,1)}, u32[]{:S(2)}) copy-start(bf16[1,128,2,128]{3,2,1,0:T(2,128)(2,1)} %param.14) | copy-start | bytes 196612
  7.2 5.2 %copy-start.1 = (bf16[1,128,256]{2,1,0:T(8,128)(2,1)S(1)}, bf16[1,128,256]{2,1,0:T(8,128)(2,1)}, u32[]{:S(2)}) copy-start(bf16[1,128,256]{2,1,0:T(8,128)(2,1)} %param.13) | copy-start | bytes 196612
  7.2 6.6 %copy-start.2 = (bf16[1,128,256]{2,1,0:T(8,128)(2,1)S(1)}, bf16[1,128,256]{2,1,0:T(8,128)(2,1)}, u32[]{:S(2)}) copy-start(bf16[1,128,256]{2,1,0:T(8,128)(2,1)} %param.15) | copy-start | bytes 196612
  7.2 6.8 %copy-start.3 = (s32[1,128]{1,0:T(1,128)S(1)}, s32[1,128]{1,0:T(1,128)}, u32[]{:S(2)}) copy-start(s32[1,128]{1,0:T(1,128)} %param.17) | copy-start | bytes 1540
  7.2 6.9 %copy-start.4 = (s32[1,512]{1,0:T(1,128)S(1)}, s32[1,512]{1,0:T(1,128)}, u32[]{:S(2)}) copy-start(s32[1,512]{1,0:T(1,128)} %param.16) | copy-start | bytes 6148
  7.2 109.6 %all-gather.5.cloned.1.call-start = ((), (), s32[]{:S(2)}) async-start(), calls=%async_computation.4 | async-start | bytes 4325376 | tf_op jit(solution)/shard_map/all_gather | solution.py:76
  8.0 163.0 %all-gather.3.cloned.1.call-start = ((), (), s32[]{:S(2)}) async-start(), calls=%async_computation.3 | async-start | bytes 9437184 | tf_op jit(solution)/shard_map/all_gather | solution.py:74
  12.2 233.6 %reduce-scatter.3.cloned.1.call-start = ((), (), s32[]{:S(2)}) async-start(), calls=%async_computation.5 | async-start | bytes 4718592 | tf_op jit(solution)/shard_map/reduce_scatter | solution.py:20
  178.5 3.4 %copy-start.5 = (bf16[512,8192]{1,0:T(8,128)(2,1)S(1)}, bf16[512,8192]{1,0:T(8,128)(2,1)}, u32[]{:S(2)}) copy-start(bf16[512,8192]{1,0:T(8,128)(2,1)} %all-gather.3.cloned.1.call-done) | copy-start | bytes 25165828
  185.8 90.7 %reduce-scatter.5.cloned.1.call-start = ((), (), s32[]{:S(2)}) async-start(), calls=%async_computation.6 | async-start | bytes 655360 | tf_op jit(solution)/shard_map/reduce_scatter | solution.py:20
  278.2 8.6 %all-to-all-start = ((bf16[2,256,2,128]{3,1,2,0:T(8,128)(2,1)}), bf16[2,256,2,128]{3,1,2,0:T(8,128)(2,1)S(1)}, u32[]{:S(2)}, u32[]{:S(2)}) async-start(bf16[2,256,2,128]{3,1,2,0:T(8,128)(2,1)} %broadcast_in_dim.24), calls=%async_computation.2 | async-start | bytes 524288 | tf_op jit(solution)/shard_map/all_to_all | solution.py:26
Sparse Core Ops, SparseCore 0:
  11.2 105.6 all-gather.4
  119.0 51.8 all-gather.2
  185.9 59.7 reduce-scatter.2
  248.4 28.1 reduce-scatter.4
where the time goes:
time: 295 us; the launch traced here: 294 us
  waiting for transfers between devices  250 us (85%)
  between operations  15.3 us (5%)
  matrix products  12.6 us (4%)
  local copies, waits for them, and re-layouts  7.58 us (3%)
  other arithmetic  4.84 us (2%)
  starting transfers between devices  3.6 us (1%)
    all_gather x1, waiting for transfers between devices, shards(): piece = lax.all_gather(kv_weight, DP, axis=0, tiled=True)  103 us
    reduce_scatter x2, waiting for transfers between devices, sum_by_axis(): subtotal = lax.psum_scatter(subtotal, axis, scatter_dimension=0, tiled=True)  89.6 us
    all_gather x1, waiting for transfers between devices, shards(): normed = lax.all_gather(normed_local, 'mp', axis=0, tiled=True)  54.1 us
    dot_general x1, matrix products, shards(): jnp.dot(section, piece.reshape(piece.shape[0], columns), preferred_elemen...  6.94 us
  transfers between devices with their start and end apart: 5, of which 5 were waited for; matrix products, arithmetic and copies ran while one was open for 3% of the time, Pallas kernels for 0%

commit v1 on v0

--- a/solution.py
+++ b/solution.py
@@ -71,7 +71,9 @@
     wide = prefix_hidden[0].astype(jnp.float32)
     inverse = lax.rsqrt(jnp.mean(wide * wide, axis=-1, keepdims=True) + EPS)
     normed_local = (wide * inverse * norm_gain).astype(jnp.bfloat16)
-    normed = lax.all_gather(normed_local, "mp", axis=0, tiled=True)
+    normed = jnp.concatenate(
+        lax.all_to_all(jnp.stack([normed_local] * lax.axis_size("mp")), "mp", 0, 0), axis=0
+    )
     rows = normed.shape[0]
     piece = lax.all_gather(kv_weight, DP, axis=0, tiled=True)
     section = normed

time: 295 us -> 244 us (0.83)
  waiting for transfers between devices: 250 us -> 187 us
  matrix products: 12.6 us -> 18.2 us
  starting transfers between devices: 3.6 us -> 9.04 us
    all_gather x1, waiting for transfers between devices: 103 us -> 2.85 us  [shards(): piece = lax.all_gather(kv_weight, DP, axis=0, tiled=True)]
    all_to_all x0 -> x1, waiting for transfers between devices: none -> 91.2 us  [shards(): lax.all_to_all(jnp.stack([normed_local] * lax.axis_size('mp')), 'mp', 0, 0)]
    all_gather x1 -> x0, waiting for transfers between devices: 54.1 us -> none  [shards(): normed = lax.all_gather(normed_local, 'mp', axis=0, tiled=True)]
    dot_general x1, matrix products: 3.96 us -> 9.58 us  [shards(): lax.dot_general(section, prefix_grad, (((0,), (0,)), ((), ())), preferred...]
    all_to_all x0 -> x1, starting transfers between devices: none -> 5.52 us  [shards(): lax.all_to_all(jnp.stack([normed_local] * lax.axis_size('mp')), 'mp', 0, 0)]
    another operation x1 -> x2, local copies, waits for them, and re-layouts: 0.11 us -> 4.34 us  [the longest x1 4.23 us: shards(): jnp.stack([normed_local] * lax.axis_size('mp'))]
  transfers between devices with their start and end apart: 5 -> 5, of which waited for: 5 -> 5; matrix products, arithmetic and copies ran while one was open for 3% -> 4% of each run, Pallas kernels for 0% -> 0%
where the time goes in v1:
time: 244 us; the launch traced here: 243 us
  waiting for transfers between devices  187 us (77%)
  matrix products  18.2 us (7%)
  between operations  15.3 us (6%)
  local copies, waits for them, and re-layouts  9.54 us (4%)
  starting transfers between devices  9.04 us (4%)
  other arithmetic  3.78 us (2%)
    all_to_all x1, waiting for transfers between devices, shards(): lax.all_to_all(jnp.stack([normed_local] * lax.axis_size('mp')), 'mp', 0, 0)  91.2 us
    reduce_scatter x2, waiting for transfers between devices, sum_by_axis(): subtotal = lax.psum_scatter(subtotal, axis, scatter_dimension=0, tiled=True)  89.4 us
    dot_general x1, matrix products, shards(): lax.dot_general(section, prefix_grad, (((0,), (0,)), ((), ())), preferred...  9.58 us
    dot_general x1, matrix products, shards(): jnp.dot(section, piece.reshape(piece.shape[0], columns), preferred_elemen...  6.94 us
    all_to_all x1, starting transfers between devices, shards(): lax.all_to_all(jnp.stack([normed_local] * lax.axis_size('mp')), 'mp', 0, 0)  5.52 us
  transfers between devices with their start and end apart: 5, of which 5 were waited for; matrix products, arithmetic and copies ran while one was open for 4% of the time, Pallas kernels for 0%

profile of v1, /device:TPU:18, one launch (start us, length us, event | category | flops | bytes accessed | tf_op | source)
XLA Modules:
  0.0 243.3 jit_solution(14769944003594882466)
XLA Ops:
  7.2 0.0 all-gather.2.cloned.1.call-start
  7.2 0.7 all-gather.2.cloned.1.call-update
  7.9 1.5 fusion.3
  9.4 1.5 fusion.13
  11.0 4.2 %stack.11 = bf16[8,64,8192]{2,1,0:T(8,128)(2,1)} broadcast(bf16[64,8192]{1,0:T(8,128)(2,1)S(1)} %fusion.13), dimensions={1,2} | broadcast | bytes 9437184 | tf_op jit(solution)/shard_map/stack | solution.py:75
  15.2 0.0 copy-start
  15.2 0.0 copy-start.1
  15.2 0.0 copy-start.2
  15.2 0.0 copy-start.3
  15.2 0.0 copy-start.4
  15.2 5.5 %all-to-all-start = ((bf16[8,64,8192]{2,1,0:T(8,128)(2,1)}), bf16[8,64,8192]{2,1,0:T(8,128)(2,1)}, u32[]{:S(2)}, u32[]{:S(2)}) async-start(bf16[8,64,8192]{2,1,0:T(8,128)(2,1)} %stack.11), calls=%async_computation | async-start | bytes 16777216 | tf_op jit(solution)/shard_map/all_to_all | solution.py:75
  20.8 0.0 reduce-scatter.3.cloned.1.call-start
  20.8 0.0 copy-done
  20.8 0.1 copy.73
  20.9 0.0 copy-done.1
  20.9 0.1 copy.101
  22.4 0.0 copy-done.2
  22.4 0.1 copy.102
  22.5 0.0 copy-done.3
  22.5 0.1 broadcast_compare_fusion
  22.6 0.0 copy-done.4
  22.6 0.2 compare_and_fusion
  22.8 91.2 %all-to-all-done = bf16[8,64,8192]{2,1,0:T(8,128)(2,1)} async-done(((bf16[8,64,8192]{2,1,0:T(8,128)(2,1)}), bf16[8,64,8192]{2,1,0:T(8,128)(2,1)}, u32[]{:S(2)}, u32[]{:S(2)}) %all-to-all-start) | async-done | bytes 8388640 | tf_op jit(solution)/shard_map/all_to_all | solution.py:75
  114.0 2.8 %all-gather.2.cloned.1.call-done = bf16[8192,2,128]{2,1,0:T(2,128)(2,1)} async-done(((bf16[256,2,128]{2,1,0:T(2,128)(2,1)}), bf16[8192,2,128]{2,1,0:T(2,128)(2,1)}) %all-gather.2.cloned.1.call-update) | async-done | bytes 4194320 | tf_op jit(solution)/shard_map/all_gather | solution.py:78
  116.9 6.9 %fusion.7 = bf16[512,256]{0,1:T(8,128)(2,1)S(1)} fusion(bf16[512,8192]{1,0:T(8,128)(2,1)} %bitcast.1, bf16[1024,8,2,128]{3,2,1,0:T(2,128)(2,1)} %bitcast.128), kind=kOutput, calls=%fused_computation.12 | convolution fusion | flops 2147614720 | bytes 12845056 | tf_op jit(solution)/shard_map/dot_general | solution.py:80
  123.9 0.1 copy.100
  124.0 0.3 fusion.33
  124.3 0.1 fusion.15
  124.4 0.3 convolution_bitcast_fusion.1
  124.7 0.3 multiply_reduce_fusion
  125.1 0.2 fusion.17
  125.3 0.2 fusion.12
  125.5 9.6 %convolution_convert_fusion = bf16[8192,2,128]{2,0,1:T(8,128)(2,1)} fusion(bf16[512,8192,1]{1,0,2:T(8,128)(2,1)} %bitcast.42, f32[640,1,1,128]{0,3,2,1:T(8,128)S(1)} %convolution_bitcast_fusion.1, f32[640,1,1,128]{0,3,2,1:T(8,128)S(1)} %fusion.12), kind=kOutput, calls=%fused_computation | convolution fusion | flops 2150105088 | bytes 13238272 | tf_op jit(solution)/shard_map/dot_general | solution.py:116
  135.1 0.0 reduce-scatter.3.cloned.1.call-update
  135.1 0.0 reduce-scatter.5.cloned.1.call-start
  135.2 59.5 %reduce-scatter.3.cloned.1.call-done = bf16[1024,2,128]{2,0,1:T(8,128)(2,1)} async-done(((bf16[8192,2,128]{2,0,1:T(8,128)(2,1)}), bf16[1024,2,128]{2,0,1:T(8,128)(2,1)}) %reduce-scatter.3.cloned.1.call-update) | async-done | bytes 524304 | tf_op jit(solution)/shard_map/reduce_scatter | solution.py:20
  194.7 0.0 reduce-scatter.5.cloned.1.call-update
  194.7 0.3 convolution_convert_fusion.1
  195.0 0.7 copy.86
  195.7 29.9 %reduce-scatter.5.cloned.1.call-done = bf16[256,2,128]{2,0,1:T(8,128)(2,1)} async-done(((bf16[1024,2,128]{2,0,1:T(8,128)(2,1)}), bf16[256,2,128]{2,0,1:T(8,128)(2,1)}) %reduce-scatter.5.cloned.1.call-update) | async-done | bytes 131088 | tf_op jit(solution)/shard_map/reduce_scatter | solution.py:20
  225.6 1.6 broadcast_in_dim.24
  227.3 3.4 %all-to-all-start.1 = ((bf16[2,256,2,128]{3,1,2,0:T(8,128)(2,1)}), bf16[2,256,2,128]{3,1,2,0:T(8,128)(2,1)S(1)}, u32[]{:S(2)}, u32[]{:S(2)}) async-start(bf16[2,256,2,128]{3,1,2,0:T(8,128)(2,1)} %broadcast_in_dim.24), calls=%async_computation.3 | async-start | bytes 524288 | tf_op jit(solution)/shard_map/all_to_all | solution.py:26
  230.7 0.3 convolution_multiply_fusion.1
  231.0 0.8 copy.87
  231.7 0.8 copy.88
  232.5 3.4 %all-to-all-done.1 = bf16[2,256,2,128]{3,1,2,0:T(8,128)(2,1)S(1)} async-done(((bf16[2,256,2,128]{3,1,2,0:T(8,128)(2,1)}), bf16[2,256,2,128]{3,1,2,0:T(8,128)(2,1)S(1)}, u32[]{:S(2)}, u32[]{:S(2)}) %all-to-all-start.1) | async-done | bytes 262176 | tf_op jit(solution)/shard_map/all_to_all | solution.py:26
  235.9 0.9 copy.89
  (10 shorter events, 0.1 us)
Async XLA Ops:
  7.2 109.7 %all-gather.2.cloned.1.call-start = ((), (), s32[]{:S(2)}) async-start(), calls=%async_computation.4 | async-start | bytes 4325376 | tf_op jit(solution)/shard_map/all_gather | solution.py:78
  15.2 5.5 %copy-start = (bf16[1,128,2,128]{3,2,1,0:T(2,128)(2,1)S(1)}, bf16[1,128,2,128]{3,2,1,0:T(2,128)(2,1)}, u32[]{:S(2)}) copy-start(bf16[1,128,2,128]{3,2,1,0:T(2,128)(2,1)} %param.14) | copy-start | bytes 196612
  15.2 5.7 %copy-start.1 = (bf16[1,128,256]{2,1,0:T(8,128)(2,1)S(1)}, bf16[1,128,256]{2,1,0:T(8,128)(2,1)}, u32[]{:S(2)}) copy-start(bf16[1,128,256]{2,1,0:T(8,128)(2,1)} %param.13) | copy-start | bytes 196612
  15.2 7.1 %copy-start.2 = (bf16[1,128,256]{2,1,0:T(8,128)(2,1)S(1)}, bf16[1,128,256]{2,1,0:T(8,128)(2,1)}, u32[]{:S(2)}) copy-start(bf16[1,128,256]{2,1,0:T(8,128)(2,1)} %param.15) | copy-start | bytes 196612
  15.2 7.3 %copy-start.3 = (s32[1,128]{1,0:T(1,128)S(1)}, s32[1,128]{1,0:T(1,128)}, u32[]{:S(2)}) copy-start(s32[1,128]{1,0:T(1,128)} %param.17) | copy-start | bytes 1540
  15.2 7.4 %copy-start.4 = (s32[1,512]{1,0:T(1,128)S(1)}, s32[1,512]{1,0:T(1,128)}, u32[]{:S(2)}) copy-start(s32[1,512]{1,0:T(1,128)} %param.16) | copy-start | bytes 6148
  15.2 98.8 %all-to-all-start = ((bf16[8,64,8192]{2,1,0:T(8,128)(2,1)}), bf16[8,64,8192]{2,1,0:T(8,128)(2,1)}, u32[]{:S(2)}, u32[]{:S(2)}) async-start(bf16[8,64,8192]{2,1,0:T(8,128)(2,1)} %stack.11), calls=%async_computation | async-start | bytes 16777216 | tf_op jit(solution)/shard_map/all_to_all | solution.py:75
  20.8 173.9 %reduce-scatter.3.cloned.1.call-start = ((), (), s32[]{:S(2)}) async-start(), calls=%async_computation.5 | async-start | bytes 4718592 | tf_op jit(solution)/shard_map/reduce_scatter | solution.py:20
  135.1 90.5 %reduce-scatter.5.cloned.1.call-start = ((), (), s32[]{:S(2)}) async-start(), calls=%async_computation.6 | async-start | bytes 655360 | tf_op jit(solution)/shard_map/reduce_scatter | solution.py:20
  227.3 8.6 %all-to-all-start.1 = ((bf16[2,256,2,128]{3,1,2,0:T(8,128)(2,1)}), bf16[2,256,2,128]{3,1,2,0:T(8,128)(2,1)S(1)}, u32[]{:S(2)}, u32[]{:S(2)}) async-start(bf16[2,256,2,128]{3,1,2,0:T(8,128)(2,1)} %broadcast_in_dim.24), calls=%async_computation.3 | async-start | bytes 524288 | tf_op jit(solution)/shard_map/all_to_all | solution.py:26
Sparse Core Ops, SparseCore 0:
  11.2 105.6 all-gather.1
  135.3 59.3 reduce-scatter.2
  197.5 28.1 reduce-scatter.4
